TPU v7x, 32 devices: a whole 2x2x4 slice. The times are simulated.
32 devices in a mesh: slab: 2 (over x), line: 8 (over z, y), band: 2 (over core).
Axes of the slice: x: 2, y: 2, z: 4, core: 2. Of those that a mesh axis runs over, the one named last changes fastest.
Arguments:
- cube: bfloat16 [230, 2048, 256], P('band', ('slab', 'line')), parts along dimension 1, may hold values from -6 to 6
- observed: bfloat16 [13, 2048, 256], P(None, ('slab', 'line')), parts along dimension 1, may hold values from -6 to 6
- along_kernels: bfloat16 [3, 128, 128], replicated, may hold values from -0.3125 to 0.3125
- along_offsets: int32 [3], replicated, may hold values from -1 to 1, as said below
- across_kernels: bfloat16 [3, 128, 128], replicated, may hold values from -0.3125 to 0.3125
- across_offsets: int32 [3], replicated, may hold values from -1 to 1, as said below
- resp_start: int32 [13], replicated, may hold values from 0 to 21
- resp_values: bfloat16 [13, 20], replicated, may hold values from 0.049804688 to 0.3984375
Outputs:
- synthetic: float32 [13, 2048, 256], P(None, ('slab', 'line')), parts along dimension 1
- angles: float32 [2048, 256], P(('slab', 'line')), parts along dimension 0
There are 2 independent parts, one for each index of `slab`. A program takes and returns all parts, laid end to end along the dimension named above; an argument that names none is the same for every part. Nothing has to cross between parts.
Inputs may be any that keep to these rules, and one draw needn't show every extreme that they name: `along_offsets`: the three entries are -1, 0 and 1, each once. `across_offsets`: the three entries are -1, 0 and 1, each once.
All inputs are finite; a program needn't handle non-finite values.
Results may differ from a plain program's by a relative error of at most 0.0003.
Values may be sent and summed in bfloat16 or wider, within the bound.
No kernel may reach another device: no remote copies, remote signals or barrier semaphores. Data moves between devices by JAX's collectives and lax.ppermute only.
A program may use at most 192 MiB of HBM per device.

v0:
```python
import jax
import jax.numpy as jnp
from jax import lax
from jax.sharding import PartitionSpec as P

BLK = 128
SPB = 10


def extended(shard, sides, width):
    for axis, dim in sides:
        size, length = (lax.axis_size(axis), shard.shape[dim])
        up = [(i, (i + 1) % size) for i in range(size - 1)]
        down = [(j, i) for i, j in up]
        last = lax.slice_in_dim(shard, length - width, length, axis=dim)
        leading = lax.slice_in_dim(shard, 0, width, axis=dim)
        before = lax.ppermute(last, axis, up)
        after = lax.ppermute(leading, axis, down)
        shard = jnp.concatenate([before, shard, after], axis=dim)
    return shard


def pick_kernels(kernels, offsets):
    shifts = jnp.arange(3, dtype=jnp.int32) - 1
    onehot = (offsets[None, :] == shifts[:, None]).astype(jnp.float32)
    return jnp.einsum(
        "sk,kpq->spq", onehot, kernels.astype(jnp.float32), precision=lax.Precision.HIGHEST
    )


def dense_response(resp_start, resp_values, band_total):
    bands = jnp.arange(band_total, dtype=jnp.int32)
    local = bands[None, :] - SPB * resp_start[:, None]
    slots = jnp.arange(2 * SPB, dtype=jnp.int32)
    hits = local[:, :, None] == slots[None, None, :]
    return jnp.sum(
        jnp.where(hits, resp_values.astype(jnp.float32)[:, None, :], jnp.float32(0.0)), axis=-1
    )


def along_blocks(padded, chosen, count):
    total = None
    for index in range(3):
        term = jnp.einsum(
            "pq,bnqc->bnpc",
            chosen[index],
            padded[:, index : index + count],
            precision=lax.Precision.HIGHEST,
        )
        total = term if total is None else total + term
    return total


def across_filter(field, chosen):
    count = field.shape[2] // BLK
    blocks = field.reshape(field.shape[0], field.shape[1], count, BLK)
    padded = jnp.pad(blocks, ((0, 0), (0, 0), (1, 1), (0, 0)))
    total = jnp.zeros(blocks.shape, jnp.float32)
    for index in range(3):
        total = total + jnp.einsum(
            "pq,blnq->blnp",
            chosen[index],
            padded[:, :, index : index + count],
            precision=lax.Precision.HIGHEST,
        )
    return total.reshape(field.shape)


def respond_plain(weights, field):
    return jnp.einsum(
        "mb,blc->mlc", weights.astype(jnp.bfloat16), field, preferred_element_type=jnp.float32
    )


def on_device(
    cube,
    observed,
    along_kernels,
    along_offsets,
    across_kernels,
    across_offsets,
    resp_start,
    resp_values,
):
    band_share = cube.shape[0]
    line_rows = cube.shape[1]
    column_count = cube.shape[2]
    band_total = band_share * lax.axis_size("band")
    along_pick = pick_kernels(along_kernels, along_offsets)
    across_pick = pick_kernels(across_kernels, across_offsets)
    response = dense_response(resp_start, resp_values, band_total)
    local_response = lax.dynamic_slice_in_dim(
        response, lax.axis_index("band") * band_share, band_share, 1
    )
    count = line_rows // BLK
    folded = respond_plain(local_response, cube)
    summed = lax.psum(folded, "band")
    padded_sum = extended(summed, (("line", 1),), BLK)
    padded = padded_sum.reshape(summed.shape[0], count + 2, BLK, column_count)
    smooth = along_blocks(padded, along_pick, count).reshape(summed.shape)
    partial_value = across_filter(smooth, across_pick)
    seen = observed.astype(jnp.float32)
    inner = jnp.sum(partial_value * seen, axis=0)
    first = jnp.sqrt(jnp.sum(partial_value * partial_value, axis=0))
    second = jnp.sqrt(jnp.sum(seen * seen, axis=0))
    angles = jnp.arccos(jnp.clip(inner / jnp.maximum(first * second, 1.0), -1.0, 1.0))
    return (partial_value, angles)


def solution(mesh):
    placed = (
        P("band", ("slab", "line"), None),
        P(None, ("slab", "line"), None),
        P(),
        P(),
        P(),
        P(),
        P(),
        P(),
    )
    return jax.shard_map(
        on_device,
        mesh=mesh,
        in_specs=placed,
        out_specs=(P(None, ("slab", "line"), None), P(("slab", "line"), None)),
        check_vma=False,
    )
```

profile of v0, /device:TPU:0, one launch (start us, length us, event | category | flops | bytes accessed | tf_op | source)
XLA Modules:
  0.0 157.3 jit_solution(8674825454620172075)
XLA Ops:
  7.2 0.7 broadcast_multiply_fusion
  8.0 0.7 convert_element_type.8
  8.7 0.1 select_reduce_fusion
  8.8 8.8 %fusion = f32[13,128,256]{2,0,1:T(8,128)} fusion(bf16[115,128,256]{2,1,0:T(8,128)(2,1)} %param.8, bf16[13,230]{1,0:T(8,128)(2,1)S(1)} %select_reduce_fusion, s32[]{:T(128)S(6)} %select_n.8), kind=kOutput, calls=%fused_computation | convolution fusion | flops 97976320 | bytes 9244676 | tf_op jit(solution)/shard_map/mb,blc->mlc/dot_general | solution.py:70
  17.6 24.0 %all-reduce.3.cloned.1.call-done = f32[13,128,256]{2,0,1:T(8,128)} async-done(((f32[13,128,256]{2,0,1:T(8,128)}), f32[13,128,256]{2,0,1:T(8,128)}) %all-reduce.3.cloned.1.call-update) | async-done | bytes 1703952 | tf_op jit(solution)/shard_map/psum | solution.py:97
  41.7 2.6 %copy.36 = f32[13,128,256]{2,1,0:T(8,128)S(1)} copy(f32[13,128,256]{2,0,1:T(8,128)} %all-reduce.3.cloned.1.call-done) | data formatting | bytes 3407872 | tf_op jit(solution)/shard_map/psum | solution.py:97
  44.3 3.8 %collective-permute-start = (f32[13,128,256]{2,1,0:T(8,128)S(1)}, f32[13,128,256]{2,1,0:T(8,128)S(1)}, u32[]{:S(2)}, u32[]{:S(2)}) collective-permute-start(f32[13,128,256]{2,1,0:T(8,128)S(1)} %copy.36), channel_id=1, source_target_pairs={{0,2},{2,4},{4,6},{6,8},{8,10},{10,12},{12,14},{1,3},{3,5},{5,7},{... | collective-permute-start | bytes 5111816 | tf_op jit(solution)/shard_map/ppermute | solution.py:17
  48.0 1.3 collective-permute-start.1
  49.4 0.3 fusion.14
  49.6 0.3 fusion.12
  49.9 0.1 fusion.29
  50.1 0.8 fusion.28
  50.8 70.5 %collective-permute-done = f32[13,128,256]{2,1,0:T(8,128)S(1)} collective-permute-done((f32[13,128,256]{2,1,0:T(8,128)S(1)}, f32[13,128,256]{2,1,0:T(8,128)S(1)}, u32[]{:S(2)}, u32[]{:S(2)}) %collective-permute-start) | collective-permute-done | bytes 1703968 | tf_op jit(solution)/shard_map/ppermute | solution.py:17
  121.3 1.0 copy.38
  122.4 1.0 copy.39
  123.4 0.6 copy-done.1
  123.9 0.7 pad_maximum_fusion
  124.7 2.6 %fusion.27 = (f32[13,1,128,256]{3,0,2,1:T(8,128)S(1)}, f32[13,1,128,256]{3,0,2,1:T(8,128)}, f32[13,1,128,256]{3,0,2,1:T(8,128)}) fusion(f32[13,3,128,256]{3,0,2,1:T(8,128)S(1)} %bitcast.67), kind=kLoop, calls=%fused_computation.37 | loop fusion | bytes 10223616 | tf_op jit(solution)/shard_map/slice | solution.py:47
  127.3 2.9 %copy.55 = f32[13,1,128,256]{2,3,0,1:T(8,128)} copy(f32[13,1,128,256]{3,0,2,1:T(8,128)} %get-tuple-element.11) | data formatting | bytes 3407872
  130.2 2.8 %copy.56 = f32[13,1,128,256]{2,3,0,1:T(8,128)} copy(f32[13,1,128,256]{3,0,2,1:T(8,128)} %get-tuple-element.12) | data formatting | bytes 3407872
  133.0 1.8 %copy.54 = f32[13,1,128,256]{2,3,0,1:T(8,128)} copy(f32[13,1,128,256]{3,0,2,1:T(8,128)S(1)} %get-tuple-element.10) | data formatting | bytes 3407872
  134.7 3.1 %fusion.6 = f32[13,256,128]{2,1,0:T(8,128)S(1)} fusion(f32[128,128,1]{1,0,2:T(8,128)S(1)} %bitcast.75, f32[13,1,128,256]{2,3,0,1:T(8,128)} %copy.55), kind=kOutput, calls=%fused_computation.9 | convolution fusion | flops 654311424 | bytes 3473408 | tf_op jit(solution)/shard_map/pq,bnqc->bnpc/dot_general | solution.py:44
  137.9 1.6 %fusion.4 = f32[13,256,128]{2,1,0:T(8,128)S(1)} fusion(f32[128,128,1]{1,0,2:T(8,128)S(1)} %bitcast.74, f32[13,1,128,256]{2,3,0,1:T(8,128)S(1)} %copy-done.3), kind=kOutput, calls=%fused_computation.7 | convolution fusion | flops 654311424 | bytes 3473408 | tf_op jit(solution)/shard_map/pq,bnqc->bnpc/dot_general | solution.py:44
  139.5 1.6 %add_add_fusion.1 = f32[13,256,128]{2,1,0:T(8,128)S(1)} fusion(f32[13,256,128]{2,1,0:T(8,128)S(1)} %fusion.4, f32[13,256,128]{2,1,0:T(8,128)S(1)} %fusion.6, f32[128,128,1]{1,0,2:T(8,128)S(1)} %bitcast.71, f32[13,1,128,256]{2,3,0,1:T(8,128)S(1)} %copy-done.4), kind=kOutput, calls=%fused_computation.15 | convolution fusion | flops 655163392 | bytes 6881280 | tf_op jit(solution)/shard_map/pq,bnqc->bnpc/dot_general | solution.py:44
  141.1 1.6 %fusion.30 = f32[13,128,2,128]{1,3,2,0:T(8,128)S(1)} fusion(f32[13,128,2,128]{1,3,2,0:T(8,128)S(1)} %bitcast.64, f32[128,128,1,1]{1,0,3,2:T(8,128)S(1)} %bitcast.73), kind=kOutput, calls=%fused_computation.40 | convolution fusion | flops 654311424 | bytes 3473408 | tf_op jit(solution)/shard_map/pq,blnq->blnp/dot_general | solution.py:60
  142.8 1.5 fusion.31
  144.3 1.8 %multiply_reduce_fusion = (f32[128,2,128]{0,2,1:T(8,128)}, f32[13,128,2,128]{1,3,2,0:T(8,128)S(1)}) fusion(f32[13,128,2,128]{1,3,2,0:T(8,128)S(1)} %bitcast.66, f32[128,128,1,1]{1,0,3,2:T(8,128)S(1)} %bitcast.70, f32[13,128,2,128]{1,3,2,0:T(8,128)S(1)} %fusion.31, f32[13,128,2,128]{1,3,2,0:T(8,128)S(1)} %fusion.30), kind=kOutput, calls=%fused_computation.13 | convolution fusion | flops 328826880 | bytes 7012352 | tf_op jit(solution)/shard_map/pq,blnq->blnp/dot_general | solution.py:60
  146.0 0.7 copy.49
  146.8 1.1 sqrt.9
  147.9 0.1 copy.48
  148.0 1.5 fusion.3
  149.5 1.0 sqrt_atan2_fusion
  (22 shorter events, 0.2 us)
Async XLA Ops:
  7.2 42.2 %copy-start = (bf16[3,128,128]{2,1,0:T(8,128)(2,1)S(1)}, bf16[3,128,128]{2,1,0:T(8,128)(2,1)}, u32[]{:S(2)}) copy-start(bf16[3,128,128]{2,1,0:T(8,128)(2,1)} %param.10) | copy-start | bytes 294916
  7.2 34.5 %all-reduce.3.cloned.1.call-start = ((), (), s32[]{:S(2)}) async-start(), calls=%async_computation | async-start | bytes 4194304 | tf_op jit(solution)/shard_map/psum | solution.py:97
  17.6 31.7 %copy-start.7 = (s32[3]{0:T(128)S(1)}, s32[3]{0:T(128)}, u32[]{:S(2)}) copy-start(s32[3]{0:T(128)} %param.11) | copy-start | bytes 40
  17.6 32.0 %copy-start.6 = (bf16[3,128,128]{2,1,0:T(8,128)(2,1)S(1)}, bf16[3,128,128]{2,1,0:T(8,128)(2,1)}, u32[]{:S(2)}) copy-start(bf16[3,128,128]{2,1,0:T(8,128)(2,1)} %param.12) | copy-start | bytes 294916
  17.6 32.0 %copy-start.8 = (s32[3]{0:T(128)S(1)}, s32[3]{0:T(128)}, u32[]{:S(2)}) copy-start(s32[3]{0:T(128)} %param.13) | copy-start | bytes 40
  44.3 77.1 %collective-permute-start = (f32[13,128,256]{2,1,0:T(8,128)S(1)}, f32[13,128,256]{2,1,0:T(8,128)S(1)}, u32[]{:S(2)}, u32[]{:S(2)}) collective-permute-start(f32[13,128,256]{2,1,0:T(8,128)S(1)} %copy.36), channel_id=1, source_target_pairs={{0,2},{2,4},{4,6},{6,8},{8,10},{10,12},{12,14},{1,3},{3,5},{5,7},{... | collective-permute-start | bytes 5111816 | tf_op jit(solution)/shard_map/ppermute | solution.py:17
  48.0 74.3 %collective-permute-start.1 = (f32[13,128,256]{2,1,0:T(8,128)S(1)}, f32[13,128,256]{2,1,0:T(8,128)S(1)}, u32[]{:S(2)}, u32[]{:S(2)}) collective-permute-start(f32[13,128,256]{2,1,0:T(8,128)S(1)} %copy.36), channel_id=1, source_target_pairs={{2,0},{4,2},{6,4},{8,6},{10,8},{12,10},{14,12},{3,1},{5,3},{7,5},{... | collective-permute-start | bytes 5111816 | tf_op jit(solution)/shard_map/ppermute | solution.py:18
  122.3 1.6 %copy-start.1 = (f32[13,128,256]{2,0,1:T(8,128)S(1)}, f32[13,128,256]{2,0,1:T(8,128)}, u32[]{:S(2)}) copy-start(f32[13,128,256]{2,0,1:T(8,128)} %all-reduce.3.cloned.1.call-done) | copy-start | bytes 5111812
  134.7 3.1 %copy-start.3 = (f32[13,1,128,256]{2,3,0,1:T(8,128)S(1)}, f32[13,1,128,256]{2,3,0,1:T(8,128)}, u32[]{:S(2)}) copy-start(f32[13,1,128,256]{2,3,0,1:T(8,128)} %copy.56) | copy-start | bytes 5111812
  137.9 1.6 %copy-start.4 = (f32[13,1,128,256]{2,3,0,1:T(8,128)S(1)}, f32[13,1,128,256]{2,3,0,1:T(8,128)}, u32[]{:S(2)}) copy-start(f32[13,1,128,256]{2,3,0,1:T(8,128)} %copy.54) | copy-start | bytes 5111812
  142.8 1.5 copy-start.5
  146.8 3.6 %copy-start.2 = (f32[13,128,256]{2,1,0:T(8,128)}, f32[13,128,256]{2,1,0:T(8,128)S(1)}, u32[]{:S(2)}) copy-start(f32[13,128,256]{2,1,0:T(8,128)S(1)} %copy.49) | copy-start | bytes 5111812
Sparse Core Ops, SparseCore 0:
  17.7 23.9 all-reduce.2
where the time goes:
time: 158 us; the launch traced here: 157 us
  waiting for transfers between devices  94.6 us (60%)
  matrix products  20.5 us (13%)
  local copies, waits for them, and re-layouts  18.1 us (11%)
  between operations  14.3 us (9%)
  starting transfers between devices  5.08 us (3%)
  other arithmetic  4.75 us (3%)
    ppermute x1, waiting for transfers between devices, extended(): before = lax.ppermute(last, axis, up)  70.5 us
    psum x1, waiting for transfers between devices, on_device(): summed = lax.psum(folded, 'band')  24 us
    dot_general x1, matrix products, respond_plain(): jnp.einsum('mb,blc->mlc', weights.astype(jnp.bfloat16), field, preferred_...  8.77 us
    unnamed x22, local copies, waits for them, and re-layouts  8.75 us
    dot_general x3, matrix products, along_blocks(): jnp.einsum('pq,bnqc->bnpc', chosen[index], padded[:, index:index + count]...  6.31 us
    dot_general x3, matrix products, across_filter(): jnp.einsum('pq,blnq->blnp', chosen[index], padded[:, :, index:index + cou...  4.89 us
    ppermute x1, starting transfers between devices, extended(): before = lax.ppermute(last, axis, up)  3.75 us
  transfers between devices with their start and end apart: 3, of which 2 were waited for; matrix products, arithmetic and copies ran while one was open for 2% of the time, Pallas kernels for 0%

commit v1 on v0

v1 whole, which is shorter than its diff:
```python
import functools

import jax
import jax.numpy as jnp
from jax import lax
from jax.experimental import pallas as pl
from jax.experimental.pallas import tpu as pltpu
from jax.sharding import PartitionSpec as P

BLK = 128
SPB = 10
STEPS = 16.0
PEAK = 32000.0


def which(offsets, shift):
    return sum(
        jnp.where(offsets[k] == shift, jnp.int32(k), jnp.int32(0)) for k in range(offsets.shape[0])
    )


def split(value):
    high = value.astype(jnp.bfloat16)
    low = (value - high.astype(jnp.float32)).astype(jnp.bfloat16)
    return high, low


def fold_kernel(start, offsets, values, blocks, cube, keep, send, weights, folded, across):
    bands, rows, cols = cube.shape
    count, window = values.shape
    half = cols // 2
    me = lax.axis_index("band")

    @pl.when(pl.program_id(0) == 0)
    def _():
        weights[...] = values[...].astype(jnp.float32)
        for r in range(2):
            mine = me if r == 0 else 1 - me
            for c in range(2):
                pick = which(offsets, c - mine)
                across[r * half : (r + 1) * half, c * half : (c + 1) * half] = blocks[pick]

    def one(m, carry):
        low = SPB * start[m] - bands * me
        inside = jnp.logical_and(low > -window, low < bands)

        @pl.when(inside)
        def _():
            row = weights[pl.ds(m, 1), :]
            band = low + lax.broadcasted_iota(jnp.int32, row.shape, 1)
            row = jnp.where(jnp.logical_and(band >= 0, band < bands), row, 0.0)
            total = jnp.zeros((rows, cols), jnp.float32)
            for j in range(window):
                at = jnp.clip(low + j, 0, bands - 1)
                total = total + row[:, j : j + 1] * cube[at].astype(jnp.float32)
            folded[m] = total

        @pl.when(jnp.logical_not(inside))
        def _():
            folded[m] = jnp.zeros((rows, cols), jnp.float32)

        return carry

    lax.fori_loop(0, count, one, 0)
    high, low = split(folded[...].reshape(count * rows, cols))
    dims = (((1,), (1,)), ((), ()))
    table = across[...]
    out = lax.dot_general(high, table, dims, preferred_element_type=jnp.float32)
    out = out + lax.dot_general(low, table, dims, preferred_element_type=jnp.float32)
    keep[...] = out[:, :half].reshape(count, rows, half)
    send[...] = out[:, half:].reshape(count, rows, half)


def fold(cube, start, values, blocks, offsets):
    bands, lines, cols = cube.shape
    count = values.shape[0]
    rows = 32
    half = cols // 2
    out = jax.ShapeDtypeStruct((count, lines, half), jnp.float32)
    smem = pl.BlockSpec(memory_space=pltpu.SMEM)
    vmem = pl.BlockSpec(memory_space=pltpu.VMEM)
    part = pl.BlockSpec((count, rows, half), lambda i: (0, i, 0))
    return pl.pallas_call(
        fold_kernel,
        grid=(lines // rows,),
        in_specs=[smem, smem, vmem, vmem, pl.BlockSpec((bands, rows, cols), lambda i: (0, i, 0))],
        out_specs=[part, part],
        out_shape=[out, out],
        scratch_shapes=[
            pltpu.VMEM(values.shape, jnp.float32),
            pltpu.VMEM((count, rows, cols), jnp.float32),
            pltpu.VMEM((cols, cols), jnp.bfloat16),
        ],
        compiler_params=pltpu.CompilerParams(vmem_limit_bytes=32 * 2**20),
        name="fold",
    )(start, offsets, values, blocks, cube)


def code_kernel(keep, other, total, message):
    count, lines, half = keep.shape
    value = keep[...] + other[...]
    total[...] = value
    largest = jnp.max(jnp.abs(value), axis=1)
    level = jnp.ceil(jnp.log2(jnp.maximum(largest, 1e-30)) * STEPS)
    factor = PEAK * jnp.exp2(level * (-1.0 / STEPS))
    coded = jnp.floor(value * factor[:, None, :] + 0.5).astype(jnp.int32)
    message[: count * lines, :] = coded.reshape(count * lines, half).astype(jnp.int16)
    extra = message.shape[0] - count * lines
    level = jnp.concatenate([level, jnp.zeros((extra - count, half), jnp.float32)], axis=0)
    message[count * lines :, :] = level.astype(jnp.int32).astype(jnp.int16)


def code(keep, other):
    count, lines, half = keep.shape
    extra = -(-count // 16) * 16
    return pl.pallas_call(
        code_kernel,
        out_shape=[
            jax.ShapeDtypeStruct(keep.shape, jnp.float32),
            jax.ShapeDtypeStruct((count * lines + extra, half), jnp.int16),
        ],
        compiler_params=pltpu.CompilerParams(vmem_limit_bytes=32 * 2**20),
        name="code",
    )(keep, other)


def arccos(x):
    size = jnp.abs(x)
    big = size > 0.5
    z = jnp.where(big, 0.5 * (1.0 - size), size * size)
    root = jnp.where(big, jnp.sqrt(z), size)
    poly = 4.2163199048e-2
    for term in (2.4181311049e-2, 4.5470025998e-2, 7.4953002686e-2, 1.6666752422e-1):
        poly = poly * z + term
    arcsin = poly * z * root + root
    pi = 3.14159265358979
    inner = jnp.where(x < 0, 0.5 * pi + arcsin, 0.5 * pi - arcsin)
    outer = jnp.where(x < 0, pi - 2.0 * arcsin, 2.0 * arcsin)
    return jnp.where(big, outer, inner)


def blur_kernel(offsets, blocks, total, near, far, observed, out):
    count, lines, half = total.shape
    me = lax.axis_index("band")
    even = lax.axis_index("line") % 2 == 0
    step = jnp.where(even, 1, -1)
    filters = jnp.concatenate(
        [blocks[which(offsets, s)] for s in (jnp.int32(0), step, -step)], axis=1
    )

    def levels(message):
        level = message[count * lines :, :].astype(jnp.int32).astype(jnp.float32)
        return jnp.exp2(level * (1.0 / STEPS)) * (1.0 / PEAK)

    near_scale, far_scale = levels(near), levels(far)

    def values(message, scale, m):
        coded = message[m * lines : (m + 1) * lines, :].astype(jnp.int32).astype(jnp.float32)
        return coded * scale[m : m + 1, :]

    inner = jnp.zeros((lines, half), jnp.float32)
    first = jnp.zeros((lines, half), jnp.float32)
    second = jnp.zeros((lines, half), jnp.float32)
    for m in range(count):
        parts = [total[m], values(near, near_scale, m), values(far, far_scale, m)]
        high, low = split(jnp.concatenate(parts, axis=0))
        both = jnp.dot(
            filters, jnp.concatenate([high, low], axis=1), preferred_element_type=jnp.float32
        )
        made = both[:, :half] + both[:, half:]
        out[m] = made
        seen = observed[m, :, pl.ds(pl.multiple_of(me * half, BLK), half)].astype(jnp.float32)
        inner = inner + made * seen
        first = first + made * made
        second = second + seen * seen
    bound = jnp.maximum(jnp.sqrt(first) * jnp.sqrt(second), 1.0)
    out[count] = arccos(jnp.clip(inner / bound, -1.0, 1.0))


def blur(total, near, far, observed, blocks, offsets):
    count, lines, half = total.shape
    smem = pl.BlockSpec(memory_space=pltpu.SMEM)
    vmem = pl.BlockSpec(memory_space=pltpu.VMEM)
    return pl.pallas_call(
        blur_kernel,
        in_specs=[smem] + [vmem] * 5,
        out_shape=jax.ShapeDtypeStruct((count + 1, lines, half), jnp.float32),
        compiler_params=pltpu.CompilerParams(vmem_limit_bytes=32 * 2**20),
        name="blur",
    )(offsets, blocks, total, near, far, observed)


def join_kernel(mine, other, image, angles):
    planes, _, half = mine.shape
    me = lax.axis_index("band")
    for part, where in ((mine, me), (other, 1 - me)):
        at = pl.ds(pl.multiple_of(where * half, BLK), half)
        image[:, :, at] = part[: planes - 1]
        angles[:, at] = part[planes - 1]


def join(mine, other):
    planes, lines, half = mine.shape
    return pl.pallas_call(
        join_kernel,
        out_shape=[
            jax.ShapeDtypeStruct((planes - 1, lines, 2 * half), jnp.float32),
            jax.ShapeDtypeStruct((lines, 2 * half), jnp.float32),
        ],
        compiler_params=pltpu.CompilerParams(vmem_limit_bytes=32 * 2**20),
        name="join",
    )(mine, other)


def on_device(
    cube,
    observed,
    along_kernels,
    along_offsets,
    across_kernels,
    across_offsets,
    resp_start,
    resp_values,
):
    size = lax.axis_size("line")
    swap = [(0, 1), (1, 0)]
    partner = [(i, i ^ 1) for i in range(size)]
    onward = [(i, i + 2) for i in range(0, size - 2, 2)] + [(i, i - 2) for i in range(3, size, 2)]
    keep, send = fold(cube, resp_start, resp_values, across_kernels, across_offsets)
    total, message = code(keep, lax.ppermute(send, "band", swap))
    near = lax.ppermute(message, "line", partner)
    far = lax.ppermute(near, "line", onward)
    mine = blur(total, near, far, observed, along_kernels, along_offsets)
    return tuple(join(mine, lax.ppermute(mine, "band", swap)))


def solution(mesh):
    placed = (
        P("band", ("slab", "line"), None),
        P(None, ("slab", "line"), None),
        P(),
        P(),
        P(),
        P(),
        P(),
        P(),
    )
    return jax.shard_map(
        on_device,
        mesh=mesh,
        in_specs=placed,
        out_specs=(P(None, ("slab", "line"), None), P(("slab", "line"), None)),
        check_vma=False,
    )
```

time: 158 us -> 49.5 us (0.31)
  waiting for transfers between devices: 94.6 us -> 23.7 us
  matrix products: 20.5 us -> 0 us
  between operations: 14.3 us -> 0.68 us
  local copies, waits for them, and re-layouts: 18.1 us -> 6.03 us
  Pallas kernels: 0 us -> 10 us
  other arithmetic: 4.75 us -> 0 us
  starting transfers between devices: 5.08 us -> 8.74 us
    ppermute x2 -> x4, waiting for transfers between devices: 70.5 us -> 23.7 us  [the longest x1 10.4 us: on_device(): near = lax.ppermute(message, 'line', partner)]
    psum x1 -> x0, waiting for transfers between devices: 24 us -> none  [on_device(): summed = lax.psum(folded, 'band')]
    dot_general x9 -> x0, matrix products: 20.5 us -> none  [the longest x1 8.77 us: respond_plain(): jnp.einsum('mb,blc->mlc', weights.astype(jnp.bfloat16), field, preferred_...]
    pallas_call x0 -> x4, Pallas kernels: none -> 10 us  [the longest x1 6.82 us: fold(): pl.pallas_call(fold_kernel, grid=(lines // rows,), in_specs=[smem, smem,...]
    ppermute x2 -> x4, starting transfers between devices: 5.04 us -> 8.74 us  [the longest x1 3.71 us: on_device(): far = lax.ppermute(near, 'line', onward)]
    slice x3 -> x0, local copies, waits for them, and re-layouts: 3.55 us -> none  [the longest x1 2.65 us: along_blocks(): padded[:, index:index + count]]
    unnamed x22 -> x16, local copies, waits for them, and re-layouts: 8.75 us -> 6.03 us
    psum x1 -> x0, local copies, waits for them, and re-layouts: 2.58 us -> none  [on_device(): summed = lax.psum(folded, 'band')]
  transfers between devices with their start and end apart: 3 -> 4, of which waited for: 2 -> 4; matrix products, arithmetic and copies ran while one was open for 2% -> 0% of each run, Pallas kernels for 0% -> 0%
where the time goes in v1:
time: 49.5 us; the launch traced here: 49.2 us
  waiting for transfers between devices  23.7 us (48%)
  Pallas kernels  10 us (20%)
  starting transfers between devices  8.74 us (18%)
  local copies, waits for them, and re-layouts  6.03 us (12%)
  between operations  0.68 us (1%)
    ppermute x1, waiting for transfers between devices, on_device(): near = lax.ppermute(message, 'line', partner)  10.4 us
    ppermute x1, waiting for transfers between devices, on_device(): far = lax.ppermute(near, 'line', onward)  8.84 us
    pallas_call x1, Pallas kernels, fold(): pl.pallas_call(fold_kernel, grid=(lines // rows,), in_specs=[smem, smem,...  6.82 us
    unnamed x16, local copies, waits for them, and re-layouts  6.03 us
    ppermute x1, starting transfers between devices, on_device(): far = lax.ppermute(near, 'line', onward)  3.71 us
    ppermute x1, starting transfers between devices, on_device(): total, message = code(keep, lax.ppermute(send, 'band', swap))  2.52 us
    ppermute x1, waiting for transfers between devices, on_device(): return tuple(join(mine, lax.ppermute(mine, 'band', swap)))  2.46 us
    ppermute x1, starting transfers between devices, on_device(): near = lax.ppermute(message, 'line', partner)  2.43 us
  transfers between devices with their start and end apart: 4, of which 4 were waited for; matrix products, arithmetic and copies ran while one was open for 0% of the time, Pallas kernels for 0%

profile of v1, /device:TPU:0, one launch (start us, length us, event | category | flops | bytes accessed | tf_op | source)
XLA Modules:
  0.0 49.2 jit_solution(7839500457770651872)
XLA Ops:
  0.6 0.0 copy-start
  0.6 3.1 %copy-done = bf16[115,128,256]{2,1,0:T(8,128)(2,1)S(1)} copy-done((bf16[115,128,256]{2,1,0:T(8,128)(2,1)S(1)}, bf16[115,128,256]{2,1,0:T(8,128)(2,1)}, u32[]{:S(2)}) %copy-start) | copy-done | bytes 7536664
  3.8 0.0 copy-start.2
  3.8 0.9 %copy-done.2 = bf16[3,128,128]{2,1,0:T(8,128)(2,1)S(1)} copy-done((bf16[3,128,128]{2,1,0:T(8,128)(2,1)S(1)}, bf16[3,128,128]{2,1,0:T(8,128)(2,1)}, u32[]{:S(2)}) %copy-start.2) | copy-done | bytes 98328
  4.7 0.0 copy-start.4
  4.7 0.7 %copy-done.4 = bf16[13,20]{1,0:T(8,128)(2,1)S(1)} copy-done((bf16[13,20]{1,0:T(8,128)(2,1)S(1)}, bf16[13,20]{1,0:T(8,128)(2,1)}, u32[]{:S(2)}) %copy-start.4) | copy-done | bytes 544
  5.4 0.0 copy-start.5
  5.4 0.7 %copy-done.5 = s32[13]{0:T(128)S(1)} copy-done((s32[13]{0:T(128)S(1)}, s32[13]{0:T(128)}, u32[]{:S(2)}) %copy-start.5) | copy-done | bytes 76
  6.0 0.0 copy-start.6
  6.0 0.7 %copy-done.6 = s32[3]{0:T(128)S(1)} copy-done((s32[3]{0:T(128)S(1)}, s32[3]{0:T(128)}, u32[]{:S(2)}) %copy-start.6) | copy-done | bytes 36
  6.7 0.0 copy-start.1
  6.7 0.0 copy-start.3
  6.7 0.0 copy-start.7
  6.7 6.8 %fold.1 = (f32[13,128,128]{2,1,0:T(8,128)S(1)}, f32[13,128,128]{2,1,0:T(8,128)S(1)}) custom-call(s32[13]{0:T(128)S(1)} %copy-done.5, s32[3]{0:T(128)S(1)} %copy-done.6, bf16[13,20]{1,0:T(8,128)(2,1)S(1)} %copy-done.4, bf16[3,128,128]{2,1,0:T(8,128)(2,1)S(1)} %copy-done.2, bf16[115,128,256]{2,1,0:T(8,128)(2,1)S(1)} %copy-done), custom_call_target="tpu_custom_call" | custom-call | tf_op jit(solution)/shard_map/fold/pallas_call | solution.py:83
  13.5 2.5 %collective-permute-start = (f32[13,128,128]{2,1,0:T(8,128)S(1)}, f32[13,128,128]{2,1,0:T(8,128)S(1)}, u32[]{:S(2)}, u32[]{:S(2)}) collective-permute-start(f32[13,128,128]{2,1,0:T(8,128)S(1)} %get-tuple-element.7), channel_id=1, source_target_pairs={{0,1},{1,0},{2,3},{3,2},{4,5},{5,4},{6,7},{7,6},{8,9},{9,8},{10,11... | collective-permute-start | bytes 2555912 | tf_op jit(solution)/shard_map/ppermute | solution.py:230
  16.0 2.0 %collective-permute-done.other = f32[13,128,128]{2,1,0:T(8,128)S(1)} collective-permute-done((f32[13,128,128]{2,1,0:T(8,128)S(1)}, f32[13,128,128]{2,1,0:T(8,128)S(1)}, u32[]{:S(2)}, u32[]{:S(2)}) %collective-permute-start) | collective-permute-done | bytes 852000 | tf_op jit(solution)/shard_map/ppermute | solution.py:230
  18.0 0.3 code.1
  18.3 2.4 %collective-permute-start.1 = (s16[1680,128]{1,0:T(8,128)(2,1)S(1)}, s16[1680,128]{1,0:T(8,128)(2,1)S(1)}, u32[]{:S(2)}, u32[]{:S(2)}) collective-permute-start(s16[1680,128]{1,0:T(8,128)(2,1)S(1)} %get-tuple-element.9), channel_id=1, source_target_pairs={{0,2},{2,0},{4,6},{6,4},{8,10},{10,8},{12,14},{14,12},{1,3},{3,1},... | collective-permute-start | bytes 1290248 | tf_op jit(solution)/shard_map/ppermute | solution.py:231
  20.8 10.4 %collective-permute-done.1.near = s16[1680,128]{1,0:T(8,128)(2,1)S(1)} collective-permute-done((s16[1680,128]{1,0:T(8,128)(2,1)S(1)}, s16[1680,128]{1,0:T(8,128)(2,1)S(1)}, u32[]{:S(2)}, u32[]{:S(2)}) %collective-permute-start.1) | collective-permute-done | bytes 430112 | tf_op jit(solution)/shard_map/ppermute | solution.py:231
  31.2 3.7 %collective-permute-start.2 = (s16[1680,128]{1,0:T(8,128)(2,1)S(1)}, s16[1680,128]{1,0:T(8,128)(2,1)S(1)}, u32[]{:S(2)}, u32[]{:S(2)}) collective-permute-start(s16[1680,128]{1,0:T(8,128)(2,1)S(1)} %collective-permute-done.1.near), channel_id=1, source_target_pairs={{0,4},{4,8},{8,12},{6,2},{10,6},{14,10},{1,5},{5,9},{9,13},{7,3},{... | collective-permute-start | bytes 1290248 | tf_op jit(solution)/shard_map/ppermute | solution.py:232
  34.9 8.8 %collective-permute-done.2.far = s16[1680,128]{1,0:T(8,128)(2,1)S(1)} collective-permute-done((s16[1680,128]{1,0:T(8,128)(2,1)S(1)}, s16[1680,128]{1,0:T(8,128)(2,1)S(1)}, u32[]{:S(2)}, u32[]{:S(2)}) %collective-permute-start.2) | collective-permute-done | bytes 430112 | tf_op jit(solution)/shard_map/ppermute | solution.py:232
  43.8 0.0 copy-done.1
  43.8 0.0 copy-done.3
  43.8 0.0 copy-done.7
  43.8 1.5 %blur.1.mine = f32[14,128,128]{2,1,0:T(8,128)S(1)} custom-call(s32[3]{0:T(128)S(1)} %copy-done.7, bf16[3,128,128]{2,1,0:T(8,128)(2,1)S(1)} %copy-done.3, f32[13,128,128]{2,1,0:T(8,128)S(1)} %get-tuple-element.8.total, s16[1680,128]{1,0:T(8,128)(2,1)S(1)} %collective-permute-done.1.near, s16[1680,128]{1,0:T(8,128)(2,1)S(1)} %collective-permute-done.2.far, ...), custom_call_target="tpu_custom_call" | custom-call | tf_op jit(solution)/shard_map/blur/pallas_call | solution.py:184
  45.2 0.1 collective-permute-start.3
  45.3 2.5 %collective-permute-done.3.other = f32[14,128,128]{2,1,0:T(8,128)S(1)} collective-permute-done((f32[14,128,128]{2,1,0:T(8,128)S(1)}, f32[14,128,128]{2,1,0:T(8,128)S(1)}, u32[]{:S(2)}, u32[]{:S(2)}) %collective-permute-start.3) | collective-permute-done | bytes 917536 | tf_op jit(solution)/shard_map/ppermute | solution.py:234
  47.8 1.4 %join.1 = (f32[13,128,256]{2,1,0:T(8,128)}, f32[128,256]{1,0:T(8,128)}) custom-call(f32[14,128,128]{2,1,0:T(8,128)S(1)} %blur.1.mine, f32[14,128,128]{2,1,0:T(8,128)S(1)} %collective-permute-done.3.other), custom_call_target="tpu_custom_call" | custom-call | tf_op jit(solution)/shard_map/join/pallas_call | solution.py:204
Async XLA Ops:
  0.6 3.1 %copy-start = (bf16[115,128,256]{2,1,0:T(8,128)(2,1)S(1)}, bf16[115,128,256]{2,1,0:T(8,128)(2,1)}, u32[]{:S(2)}) copy-start(bf16[115,128,256]{2,1,0:T(8,128)(2,1)} %cube.1) | copy-start | bytes 22609924
  3.8 0.9 %copy-start.2 = (bf16[3,128,128]{2,1,0:T(8,128)(2,1)S(1)}, bf16[3,128,128]{2,1,0:T(8,128)(2,1)}, u32[]{:S(2)}) copy-start(bf16[3,128,128]{2,1,0:T(8,128)(2,1)} %blocks.2) | copy-start | bytes 294916
  4.7 0.7 %copy-start.4 = (bf16[13,20]{1,0:T(8,128)(2,1)S(1)}, bf16[13,20]{1,0:T(8,128)(2,1)}, u32[]{:S(2)}) copy-start(bf16[13,20]{1,0:T(8,128)(2,1)} %values.1) | copy-start | bytes 1564
  5.4 0.7 %copy-start.5 = (s32[13]{0:T(128)S(1)}, s32[13]{0:T(128)}, u32[]{:S(2)}) copy-start(s32[13]{0:T(128)} %start.1) | copy-start | bytes 160
  6.0 0.7 %copy-start.6 = (s32[3]{0:T(128)S(1)}, s32[3]{0:T(128)}, u32[]{:S(2)}) copy-start(s32[3]{0:T(128)} %offsets.2) | copy-start | bytes 40
  6.7 37.1 %copy-start.1 = (bf16[13,128,256]{2,1,0:T(8,128)(2,1)S(1)}, bf16[13,128,256]{2,1,0:T(8,128)(2,1)}, u32[]{:S(2)}) copy-start(bf16[13,128,256]{2,1,0:T(8,128)(2,1)} %observed.1) | copy-start | bytes 2555908
  6.7 37.1 %copy-start.3 = (bf16[3,128,128]{2,1,0:T(8,128)(2,1)S(1)}, bf16[3,128,128]{2,1,0:T(8,128)(2,1)}, u32[]{:S(2)}) copy-start(bf16[3,128,128]{2,1,0:T(8,128)(2,1)} %blocks.3) | copy-start | bytes 294916
  6.7 37.1 %copy-start.7 = (s32[3]{0:T(128)S(1)}, s32[3]{0:T(128)}, u32[]{:S(2)}) copy-start(s32[3]{0:T(128)} %offsets.3) | copy-start | bytes 40
  13.5 4.5 %collective-permute-start = (f32[13,128,128]{2,1,0:T(8,128)S(1)}, f32[13,128,128]{2,1,0:T(8,128)S(1)}, u32[]{:S(2)}, u32[]{:S(2)}) collective-permute-start(f32[13,128,128]{2,1,0:T(8,128)S(1)} %get-tuple-element.7), channel_id=1, source_target_pairs={{0,1},{1,0},{2,3},{3,2},{4,5},{5,4},{6,7},{7,6},{8,9},{9,8},{10,11... | collective-permute-start | bytes 2555912 | tf_op jit(solution)/shard_map/ppermute | solution.py:230
  18.3 12.9 %collective-permute-start.1 = (s16[1680,128]{1,0:T(8,128)(2,1)S(1)}, s16[1680,128]{1,0:T(8,128)(2,1)S(1)}, u32[]{:S(2)}, u32[]{:S(2)}) collective-permute-start(s16[1680,128]{1,0:T(8,128)(2,1)S(1)} %get-tuple-element.9), channel_id=1, source_target_pairs={{0,2},{2,0},{4,6},{6,4},{8,10},{10,8},{12,14},{14,12},{1,3},{3,1},... | collective-permute-start | bytes 1290248 | tf_op jit(solution)/shard_map/ppermute | solution.py:231
  31.2 12.6 %collective-permute-start.2 = (s16[1680,128]{1,0:T(8,128)(2,1)S(1)}, s16[1680,128]{1,0:T(8,128)(2,1)S(1)}, u32[]{:S(2)}, u32[]{:S(2)}) collective-permute-start(s16[1680,128]{1,0:T(8,128)(2,1)S(1)} %collective-permute-done.1.near), channel_id=1, source_target_pairs={{0,4},{4,8},{8,12},{6,2},{10,6},{14,10},{1,5},{5,9},{9,13},{7,3},{... | collective-permute-start | bytes 1290248 | tf_op jit(solution)/shard_map/ppermute | solution.py:232
  45.2 2.5 %collective-permute-start.3 = (f32[14,128,128]{2,1,0:T(8,128)S(1)}, f32[14,128,128]{2,1,0:T(8,128)S(1)}, u32[]{:S(2)}, u32[]{:S(2)}) collective-permute-start(f32[14,128,128]{2,1,0:T(8,128)S(1)} %blur.1.mine), channel_id=1, source_target_pairs={{0,1},{1,0},{2,3},{3,2},{4,5},{5,4},{6,7},{7,6},{8,9},{9,8},{10,11... | collective-permute-start | bytes 2752520 | tf_op jit(solution)/shard_map/ppermute | solution.py:234
